TPU v7x, 256 devices: a whole 4x4x8 slice. The times are simulated.
256 devices in a mesh: ctx: 32 (over x, y, core), tp: 8 (over z).
Axes of the slice: x: 4, y: 4, z: 8, core: 2. Of those that a mesh axis runs over, the one named last changes fastest.
Arguments:
- q_in: bfloat16 [4096, 8192], P('ctx', 'tp'), may hold values from -6 to 6
- k_in: bfloat16 [4096, 8192], P('ctx', 'tp'), may hold values from -6 to 6
- v_in: bfloat16 [4096, 8192], P('ctx', 'tp'), may hold values from -6 to 6
- short_filter: float32 [3, 3, 8192], P(None, None, 'tp'), may hold values from -3 to 3
- rate: float32 [8192, 16], P('tp'), may hold values from 2.4414063e-05 to 0.05
- residue: float32 [8192, 16], P('tp'), may hold values from -0.3125 to 0.3125
- resid: bfloat16 [4096, 8192], P('ctx', 'tp'), may hold values from -18 to 18, as said below
- gain: float32 [8192], P('tp'), may hold values from 0.5 to 1.5
Outputs:
- normed: bfloat16 [4096, 8192], P('ctx', 'tp')
Inputs may be any that keep to these rules, and one draw needn't show every extreme that they name: `resid`: residual stream entries; channel scales differ across the width.
All inputs are finite; a program needn't handle non-finite values.
Results may differ from a plain program's by a relative error of at most 0.0042.
Values may be sent and summed in bfloat16 or wider, within the bound.
A program may use at most 64 MiB of HBM per device.

v0:
```python
import math

import jax
import jax.numpy as jnp
from jax import lax
from jax.sharding import PartitionSpec as P

D = 8192


def from_behind(block, axis, distance):
    devices = range(lax.axis_size(axis))
    route = [(i - distance, i) for i in devices if i - distance in devices]
    return lax.ppermute(block, axis, route)


def tables(size, outer, total):
    left = jnp.arange(size, dtype=jnp.int32)
    right = jnp.arange(outer, dtype=jnp.int32)
    phase = (left[:, None] * right[None, :] % total).astype(jnp.float32) * (2.0 * math.pi / total)
    return (jnp.cos(phase), -jnp.sin(phase))


def mat_in(table, values):
    return jnp.einsum("kn,cnm->ckm", table, values, precision=lax.Precision.HIGHEST)


def mat_out(values, table):
    return jnp.einsum("ckn,nm->ckm", values, table, precision=lax.Precision.HIGHEST)


def forward_dft(signal, first, second):
    chans = signal.shape[0]
    grid = signal.reshape(chans, first, second)
    a_re, a_im = tables(first, first, first)
    t_re, t_im = tables(first, second, first * second)
    b_re, b_im = tables(second, second, second)
    y_re = mat_in(a_re, grid)
    y_im = mat_in(a_im, grid)
    y_re, y_im = (y_re * t_re - y_im * t_im, y_re * t_im + y_im * t_re)
    f_re = mat_out(y_re, b_re) - mat_out(y_im, b_im)
    f_im = mat_out(y_re, b_im) + mat_out(y_im, b_re)
    return (f_re, f_im)


def inverse_dft(f_re, f_im, first, second):
    chans = f_re.shape[0]
    a_re, a_im = tables(first, first, first)
    t_re, t_im = tables(first, second, first * second)
    b_re, b_im = tables(second, second, second)
    z_re = mat_out(f_re, b_re) + mat_out(f_im, b_im)
    z_im = mat_out(f_im, b_re) - mat_out(f_re, b_im)
    z_re, z_im = (z_re * t_re + z_im * t_im, z_im * t_re - z_re * t_im)
    signal = mat_in(a_re.T, z_re) + mat_in(a_im.T, z_im)
    return signal.reshape(chans, first * second) / (first * second)


def spectral_conv(columns, rates, weights):
    chans, length = columns.shape
    total = 2 * length
    first = 128
    second = total // first
    times = jnp.arange(length, dtype=jnp.int32).astype(jnp.float32)
    filt = jnp.zeros((chans, length), jnp.float32)
    for m in range(rates.shape[1]):
        filt = filt + weights[:, m : m + 1] * jnp.exp(-rates[:, m : m + 1] * times[None, :])
    g_re, g_im = forward_dft(jnp.pad(columns, ((0, 0), (0, length))), first, second)
    h_re, h_im = forward_dft(jnp.pad(filt, ((0, 0), (0, length))), first, second)
    p_re = g_re * h_re - g_im * h_im
    p_im = g_re * h_im + g_im * h_re
    return inverse_dft(p_re, p_im, first, second)[:, :length]


def per_device(q_in, k_in, v_in, short_filter, rate, residue, resid, gain):
    rows, width = q_in.shape
    taps = short_filter.shape[1]
    stacked = jnp.stack([q_in, k_in, v_in])
    tail = stacked[:, rows - (taps - 1) :, :]
    before = from_behind(tail, "ctx", 1)
    padded = jnp.concatenate([before, stacked], axis=1).astype(jnp.float32)
    feats = short_filter[:, 0, None, :] * padded[:, taps - 1 :, :]
    for j in range(1, taps):
        feats = (
            feats + short_filter[:, j, None, :] * padded[:, taps - 1 - j : taps - 1 - j + rows, :]
        )
    q_feat = feats[0]
    gated = (feats[1] * feats[2]).astype(jnp.bfloat16)
    n_ctx = lax.axis_size("ctx")
    owned = width // n_ctx
    columns = lax.all_to_all(gated, "ctx", split_axis=1, concat_axis=0, tiled=True)
    start = lax.axis_index("ctx") * owned
    my_rate = lax.dynamic_slice_in_dim(rate, start, owned, 0)
    my_weight = lax.dynamic_slice_in_dim(residue, start, owned, 0)
    convolved = spectral_conv(columns.astype(jnp.float32).T, my_rate, my_weight)
    mixed = lax.all_to_all(convolved.T, "ctx", split_axis=0, concat_axis=1, tiled=True)
    stream = resid.astype(jnp.float32) + q_feat * mixed
    squares = lax.psum(jnp.sum(stream * stream, axis=1), "tp")
    scale = lax.rsqrt(squares / D + 1e-05)
    return (stream * scale[:, None] * gain[None, :]).astype(jnp.bfloat16)


def solution(mesh):
    in_specs = (
        P("ctx", "tp"),
        P("ctx", "tp"),
        P("ctx", "tp"),
        P(None, None, "tp"),
        P("tp", None),
        P("tp", None),
        P("ctx", "tp"),
        P("tp"),
    )
    out_specs = P("ctx", "tp")
    return jax.shard_map(
        per_device, mesh=mesh, in_specs=in_specs, out_specs=out_specs, check_vma=False
    )
```

profile of v0, /device:TPU:1, one launch (start us, length us, event | category | flops | bytes accessed | tf_op | source)
XLA Modules:
  0.0 103.2 jit_solution(17480730209116047577)
XLA Ops:
  0.0 1.1 %copy.22 = bf16[128,1024]{0,1:T(8,128)(2,1)S(1)} copy(bf16[128,1024]{1,0:T(8,128)(2,1)} %param.8) | data formatting | bytes 524288 | tf_op args[0]
  1.1 1.1 %copy.23 = bf16[128,1024]{0,1:T(8,128)(2,1)S(1)} copy(bf16[128,1024]{1,0:T(8,128)(2,1)} %param.9) | data formatting | bytes 524288 | tf_op args[1]
  2.3 1.2 %copy.24 = bf16[128,1024]{0,1:T(8,128)(2,1)S(1)} copy(bf16[128,1024]{1,0:T(8,128)(2,1)} %param.10) | data formatting | bytes 524288 | tf_op args[2]
  3.5 0.3 pad_maximum_fusion
  3.8 0.3 copy.25
  4.1 4.6 %collective-permute-start = (bf16[3,2,1024]{2,1,0:T(2,128)(2,1)S(1)}, bf16[3,2,1024]{2,1,0:T(2,128)(2,1)S(1)}, u32[]{:S(2)}, u32[]{:S(2)}) collective-permute-start(bf16[3,2,1024]{2,1,0:T(2,128)(2,1)S(1)} %copy.25), channel_id=1, source_target_pairs={{0,8},{8,16},{16,24},{24,32},{32,40},{40,48},{48,56},{56,64},{64,7... | collective-permute-start | bytes 36872 | tf_op jit(solution)/shard_map/ppermute | solution.py:14
  8.7 1.5 %fusion.90 = (f32[32]{0:T(128)S(1)}, f32[32]{0:T(128)S(1)}, f32[32]{0:T(128)S(1)}, f32[32]{0:T(128)S(1)}, f32[32]{0:T(128)S(1)}, /*index=5*/f32[32]{0:T(128)S(1)...) fusion(f32[1024,16]{0,1:T(8,128)} %param.12, ...), kind=kLoop, calls=%fused_computation.156 | loop fusion | flops 512 | bytes 8256 | tf_op jit(solution)/shard_map/mul | solution.py:66
  10.2 1.6 %multiply_add_fusion.3 = f32[32,4096]{1,0:T(8,128)S(1)} fusion(f32[32]{0:T(128)S(1)} %get-tuple-element.38, f32[32]{0:T(128)S(1)} %get-tuple-element.42, f32[32]{0:T(128)S(1)} %get-tuple-element.24, f32[32]{0:T(128)S(1)} %get-tuple-element.56, f32[32]{0:T(128)S(1)} %get-tuple-element.25, f32[32]{0:T(128)S(1)} %get-tuple-element.55, ...), kind=kLoop, calls=%fused_computation.43 | loop fusion | flops 6160384 | bytes 544768 | tf_op jit(solution)/shard_map/add | solution.py:66
  11.9 0.8 reshape.69
  12.8 1.3 %copy-done = f32[32,128,64]{2,1,0:T(8,128)} copy-done((f32[32,128,64]{2,1,0:T(8,128)}, f32[32,128,64]{2,1,0:T(8,128)S(1)}, u32[]{:S(2)}) %copy-start) | copy-done | bytes 1048600
  14.1 3.5 %convolution_bitcast_fusion = f32[32,128,64]{1,2,0:T(8,128)S(1)} fusion(f32[32,128,64]{2,1,0:T(8,128)S(1)} %reshape.69), kind=kOutput, calls=%fused_computation.14 | convolution fusion | flops 402898944 | bytes 2097152 | tf_op jit(solution)/shard_map/kn,cnm->ckm/dot_general | solution.py:25
  17.6 5.1 %convolution_bitcast_fusion.1 = f32[32,128,64]{1,2,0:T(8,128)S(1)} fusion(f32[32,128,64]{2,1,0:T(8,128)} %copy-done), kind=kOutput, calls=%fused_computation.15 | convolution fusion | flops 402882560 | bytes 2097152 | tf_op jit(solution)/shard_map/kn,cnm->ckm/dot_general | solution.py:25
  22.6 0.1 sine_negate_fusion.5
  22.8 1.3 %fusion.21 = f32[32,128,64]{1,2,0:T(8,128)S(1)} fusion(f32[32,128,64]{1,2,0:T(8,128)S(1)} %convolution_bitcast_fusion, f32[32,128,64]{1,2,0:T(8,128)S(1)} %convolution_bitcast_fusion.1, f32[128,64]{0,1:T(8,128)S(1)} %get-tuple-element.58, f32[128,64]{0,1:T(8,128)S(1)} %get-tuple-element.59), kind=kOutput, calls=%fused_computation.51 | convolution fusion | flops 202170368 | bytes 3211264 | tf_op jit(solution)/shard_map/ckn,nm->ckm/dot_general | solution.py:29
  24.1 1.3 %fusion.20 = f32[32,128,64]{1,2,0:T(8,128)S(1)} fusion(f32[32,128,64]{1,2,0:T(8,128)S(1)} %convolution_bitcast_fusion, f32[32,128,64]{1,2,0:T(8,128)S(1)} %convolution_bitcast_fusion.1, f32[128,64]{0,1:T(8,128)S(1)} %get-tuple-element.58, f32[128,64]{0,1:T(8,128)S(1)} %get-tuple-element.59), kind=kOutput, calls=%fused_computation.50 | convolution fusion | flops 202174464 | bytes 3211264 | tf_op jit(solution)/shard_map/ckn,nm->ckm/dot_general | solution.py:29
  25.5 2.5 %convolution_subtract_fusion.1 = f32[32,128,64]{1,2,0:T(8,128)} fusion(f32[32,128,64]{1,2,0:T(8,128)S(1)} %fusion.21, f32[32,128,64]{1,2,0:T(8,128)S(1)} %convolution_bitcast_fusion, f32[32,128,64]{1,2,0:T(8,128)S(1)} %convolution_bitcast_fusion.1, f32[128,64]{0,1:T(8,128)S(1)} %get-tuple-element.58, f32[128,64]{0,1:T(8,128)S(1)} %get-tuple-element.59), kind=kOutput, calls=%fused_computation.13 | convolution fusion | flops 202436608 | bytes 4259840 | tf_op jit(solution)/shard_map/ckn,nm->ckm/dot_general | solution.py:29
  28.0 1.3 %copy.26 = bf16[3,2,1024]{1,2,0:T(8,128)(2,1)} copy(bf16[3,2,1024]{2,1,0:T(2,128)(2,1)S(1)} %collective-permute-done) | data formatting | bytes 24576 | tf_op jit(solution)/shard_map/ppermute | solution.py:14
  29.3 1.9 %maximum_convert_fusion = f32[3,130,1024]{1,2,0:T(8,128)S(1)} fusion(bf16[1,128,1024]{1,2,0:T(8,128)(2,1)} %bitcast.172, bf16[1,128,1024]{1,2,0:T(8,128)(2,1)} %bitcast.170, bf16[1,128,1024]{1,2,0:T(8,128)(2,1)S(1)} %bitcast.168, bf16[3,2,1024]{1,2,0:T(8,128)(2,1)} %copy.26), kind=kLoop, calls=%fused_computation.5 | loop fusion | flops 3194880 | bytes 2396160 | tf_op jit(solution)/shard_map/convert_element_type | solution.py:80
  31.2 2.4 %fusion = f32[3,128,1024]{1,2,0:T(8,128)S(1)} fusion(f32[3,130,1024]{1,2,0:T(8,128)S(1)} %maximum_convert_fusion, f32[3,1024]{1,0:T(4,128)S(1)} %get-tuple-element.60, f32[3,1024]{1,0:T(4,128)S(1)} %get-tuple-element.61, f32[3,1024]{1,0:T(4,128)S(1)} %bitcast.173), kind=kLoop, calls=%fused_computation.1 | loop fusion | flops 1966080 | bytes 6328320 | tf_op jit(solution)/shard_map/add | solution.py:84
  33.5 1.2 %copy-done.1 = f32[3,128,1024]{1,2,0:T(8,128)} copy-done((f32[3,128,1024]{1,2,0:T(8,128)}, f32[3,128,1024]{1,2,0:T(8,128)S(1)}, u32[]{:S(2)}) %copy-start.1) | copy-done | bytes 1572888
  34.7 0.8 fusion.11
  35.4 6.7 %all-to-all-start = ((bf16[128,32,32]{0,2,1:T(8,128)(2,1)}), bf16[128,32,32]{0,2,1:T(8,128)(2,1)S(1)}, u32[]{:S(2)}, u32[]{:S(2)}) async-start(bf16[128,32,32]{0,2,1:T(8,128)(2,1)} %bitcast.4), calls=%async_computation | async-start | bytes 524288 | tf_op jit(solution)/shard_map/all_to_all | solution.py:90
  42.1 2.3 %convolution_add_fusion.2 = f32[32,128,64]{1,2,0:T(8,128)} fusion(f32[32,128,64]{1,2,0:T(8,128)S(1)} %fusion.20, f32[32,128,64]{1,2,0:T(8,128)S(1)} %convolution_bitcast_fusion, f32[32,128,64]{1,2,0:T(8,128)S(1)} %convolution_bitcast_fusion.1, f32[128,64]{0,1:T(8,128)S(1)} %get-tuple-element.58, f32[128,64]{0,1:T(8,128)S(1)} %get-tuple-element.59), kind=kOutput, calls=%fused_computation.11 | convolution fusion | flops 202432512 | bytes 4259840 | tf_op jit(solution)/shard_map/ckn,nm->ckm/dot_general | solution.py:29
  44.4 6.7 %all-to-all-done = bf16[128,32,32]{0,2,1:T(8,128)(2,1)S(1)} async-done(((bf16[128,32,32]{0,2,1:T(8,128)(2,1)}), bf16[128,32,32]{0,2,1:T(8,128)(2,1)S(1)}, u32[]{:S(2)}, u32[]{:S(2)}) %all-to-all-start) | async-done | bytes 262176 | tf_op jit(solution)/shard_map/all_to_all | solution.py:90
  51.2 1.1 %reshape.67 = bf16[32,128,64]{2,1,0:T(8,128)(2,1)S(1)} reshape(bf16[32,8192]{1,0:T(8,128)(2,1)S(1)} %pad.8) | data formatting | bytes 1048576 | tf_op jit(solution)/shard_map/reshape | solution.py:34
  52.3 1.1 %convolution_bitcast_fusion.2 = f32[32,128,64]{1,2,0:T(8,128)S(1)} fusion(bf16[32,128,64]{2,1,0:T(8,128)(2,1)S(1)} %reshape.67), kind=kOutput, calls=%fused_computation.17 | convolution fusion | flops 402898944 | bytes 1572864 | tf_op jit(solution)/shard_map/kn,cnm->ckm/dot_general | solution.py:25
  53.5 1.1 %convolution_bitcast_fusion.3 = f32[32,128,64]{1,2,0:T(8,128)S(1)} fusion(bf16[32,128,64]{2,1,0:T(8,128)(2,1)S(1)} %reshape.67), kind=kOutput, calls=%fused_computation.18 | convolution fusion | flops 402882560 | bytes 1572864 | tf_op jit(solution)/shard_map/kn,cnm->ckm/dot_general | solution.py:25
  54.6 1.3 %fusion.19 = f32[32,128,64]{1,2,0:T(8,128)S(1)} fusion(f32[32,128,64]{1,2,0:T(8,128)S(1)} %convolution_bitcast_fusion.2, f32[32,128,64]{1,2,0:T(8,128)S(1)} %convolution_bitcast_fusion.3, f32[128,64]{0,1:T(8,128)S(1)} %get-tuple-element.58, f32[128,64]{0,1:T(8,128)S(1)} %get-tuple-element.59), kind=kOutput, calls=%fused_computation.49 | convolution fusion | flops 202170368 | bytes 3211264 | tf_op jit(solution)/shard_map/ckn,nm->ckm/dot_general | solution.py:29
  55.9 1.3 %fusion.18 = f32[32,128,64]{1,2,0:T(8,128)S(1)} fusion(f32[32,128,64]{1,2,0:T(8,128)S(1)} %convolution_bitcast_fusion.2, f32[32,128,64]{1,2,0:T(8,128)S(1)} %convolution_bitcast_fusion.3, f32[128,64]{0,1:T(8,128)S(1)} %get-tuple-element.58, f32[128,64]{0,1:T(8,128)S(1)} %get-tuple-element.59), kind=kOutput, calls=%fused_computation.48 | convolution fusion | flops 202174464 | bytes 3211264 | tf_op jit(solution)/shard_map/ckn,nm->ckm/dot_general | solution.py:29
  57.3 1.3 %convolution_subtract_fusion.2 = f32[32,128,64]{1,2,0:T(8,128)S(1)} fusion(f32[32,128,64]{1,2,0:T(8,128)S(1)} %fusion.19, f32[32,128,64]{1,2,0:T(8,128)S(1)} %convolution_bitcast_fusion.2, f32[32,128,64]{1,2,0:T(8,128)S(1)} %convolution_bitcast_fusion.3, f32[128,64]{0,1:T(8,128)S(1)} %get-tuple-element.58, f32[128,64]{0,1:T(8,128)S(1)} %get-tuple-element.59), kind=kOutput, calls=%fused_computation.16 | convolution fusion | flops 202436608 | bytes 4259840 | tf_op jit(solution)/shard_map/ckn,nm->ckm/dot_general | solution.py:29
  58.6 0.2 copy-done.4
  58.8 1.7 %multiply_subtract_fusion = (f32[32,128,64]{1,2,0:T(8,128)S(1)}, f32[32,128,64]{1,2,0:T(8,128)S(1)}) fusion(f32[32,128,64]{1,2,0:T(8,128)S(1)} %copy-done.4, f32[32,128,64]{1,2,0:T(8,128)S(1)} %convolution_subtract_fusion.2, f32[32,128,64]{1,2,0:T(8,128)S(1)} %copy-done.3, f32[32,128,64]{1,2,0:T(8,128)S(1)} %fusion.18, ...), kind=kOutput, calls=%fused_computation.27 | convolution fusion | flops 204005376 | bytes 8454144 | tf_op jit(solution)/shard_map/ckn,nm->ckm/dot_general | solution.py:29
  60.5 1.2 %fusion.48 = f32[32,128,64]{1,2,0:T(8,128)S(1)} fusion(f32[32,128,64]{1,2,0:T(8,128)S(1)} %get-tuple-element.5), kind=kOutput, calls=%fused_computation.89 | convolution fusion | flops 201383936 | bytes 2097152 | tf_op jit(solution)/shard_map/ckn,nm->ckm/dot_general | solution.py:29
  61.7 1.4 %fusion.46 = f32[32,128,64]{1,2,0:T(8,128)S(1)} fusion(f32[32,128,64]{1,2,0:T(8,128)S(1)} %get-tuple-element.6), kind=kOutput, calls=%fused_computation.87 | convolution fusion | flops 201383936 | bytes 2097152 | tf_op jit(solution)/shard_map/ckn,nm->ckm/dot_general | solution.py:29
  63.1 1.2 %convolution_add_fusion.1 = f32[32,128,64]{1,2,0:T(8,128)S(1)} fusion(f32[32,128,64]{1,2,0:T(8,128)S(1)} %fusion.48, f32[32,128,64]{1,2,0:T(8,128)S(1)} %get-tuple-element.6), kind=kOutput, calls=%fused_computation.10 | convolution fusion | flops 201650176 | bytes 3145728 | tf_op jit(solution)/shard_map/ckn,nm->ckm/dot_general | solution.py:29
  64.3 1.2 %convolution_subtract_fusion = f32[32,128,64]{1,2,0:T(8,128)S(1)} fusion(f32[32,128,64]{1,2,0:T(8,128)S(1)} %fusion.46, f32[32,128,64]{1,2,0:T(8,128)S(1)} %get-tuple-element.5), kind=kOutput, calls=%fused_computation.9 | convolution fusion | flops 201650176 | bytes 3145728 | tf_op jit(solution)/shard_map/ckn,nm->ckm/dot_general | solution.py:29
  65.5 1.2 %fusion.7 = f32[32,64,128]{2,1,0:T(8,128)S(1)} fusion(f32[32,128,64]{1,2,0:T(8,128)S(1)} %convolution_subtract_fusion, f32[32,128,64]{1,2,0:T(8,128)S(1)} %convolution_add_fusion.1, f32[128,64]{0,1:T(8,128)S(1)} %get-tuple-element.58, f32[128,64]{0,1:T(8,128)S(1)} %get-tuple-element.59), kind=kOutput, calls=%fused_computation.22 | convolution fusion | flops 403668992 | bytes 3211264 | tf_op jit(solution)/shard_map/kn,cnm->ckm/dot_general | solution.py:25
  66.7 1.2 %fusion.3 = f32[32,128,64]{1,2,0:T(8,128)S(1)} fusion(f32[32,64,128]{2,1,0:T(8,128)S(1)} %fusion.7, f32[32,128,64]{1,2,0:T(8,128)S(1)} %convolution_add_fusion.1, f32[32,128,64]{1,2,0:T(8,128)S(1)} %convolution_subtract_fusion, f32[128,64]{0,1:T(8,128)S(1)} %get-tuple-element.58, f32[128,64]{0,1:T(8,128)S(1)} %get-tuple-element.59), kind=kOutput, calls=%fused_computation.8 | convolution fusion | flops 404209664 | bytes 4259840 | tf_op jit(solution)/shard_map/kn,cnm->ckm/dot_general | solution.py:25
  68.0 0.6 copy.32
  68.6 0.7 div.19
  69.2 0.9 copy_bitcast_fusion
  70.1 3.9 %all-to-all-start.1 = ((f32[32,128,32]{1,2,0:T(8,128)}), f32[32,128,32]{1,2,0:T(8,128)S(1)}, u32[]{:S(2)}, u32[]{:S(2)}) async-start(f32[32,128,32]{1,2,0:T(8,128)} %copy_bitcast_fusion), calls=%async_computation.1 | async-start | bytes 1048576 | tf_op jit(solution)/shard_map/all_to_all | solution.py:95
  74.0 0.2 copy.21
  74.2 11.5 %all-to-all-done.1 = f32[32,128,32]{1,2,0:T(8,128)S(1)} async-done(((f32[32,128,32]{1,2,0:T(8,128)}), f32[32,128,32]{1,2,0:T(8,128)S(1)}, u32[]{:S(2)}, u32[]{:S(2)}) %all-to-all-start.1) | async-done | bytes 524320 | tf_op jit(solution)/shard_map/all_to_all | solution.py:95
  85.7 0.2 multiply_reduce_fusion
  85.9 16.2 %psum.7 = f32[128]{0:T(128)S(1)} all-reduce(f32[128]{0:T(128)S(1)} %multiply_reduce_fusion), channel_id=1, replica_groups=mesh['ctx'=32,'tp'=8] {'tp'}, use_global_device_ids=true, to_apply=%region_1.2 | all-reduce | flops 128 | bytes 1024 | tf_op jit(solution)/shard_map/psum | solution.py:97
  102.1 0.2 multiply_convert_fusion
  102.3 0.9 copy.34
  (26 shorter events, 0.2 us)
Async XLA Ops:
  2.3 7.9 %copy-start.5 = (bf16[128,1024]{0,1:T(8,128)(2,1)}, bf16[128,1024]{0,1:T(8,128)(2,1)S(1)}, u32[]{:S(2)}) copy-start(bf16[128,1024]{0,1:T(8,128)(2,1)S(1)} %copy.23) | copy-start | bytes 786436
  3.5 8.4 %copy-start.6 = (bf16[128,1024]{0,1:T(8,128)(2,1)}, bf16[128,1024]{0,1:T(8,128)(2,1)S(1)}, u32[]{:S(2)}) copy-start(bf16[128,1024]{0,1:T(8,128)(2,1)S(1)} %copy.24) | copy-start | bytes 786436
  4.1 23.9 %collective-permute-start = (bf16[3,2,1024]{2,1,0:T(2,128)(2,1)S(1)}, bf16[3,2,1024]{2,1,0:T(2,128)(2,1)S(1)}, u32[]{:S(2)}, u32[]{:S(2)}) collective-permute-start(bf16[3,2,1024]{2,1,0:T(2,128)(2,1)S(1)} %copy.25), channel_id=1, source_target_pairs={{0,8},{8,16},{16,24},{24,32},{32,40},{40,48},{48,56},{56,64},{64,7... | collective-permute-start | bytes 36872 | tf_op jit(solution)/shard_map/ppermute | solution.py:14
  12.8 1.3 %copy-start = (f32[32,128,64]{2,1,0:T(8,128)}, f32[32,128,64]{2,1,0:T(8,128)S(1)}, u32[]{:S(2)}) copy-start(f32[32,128,64]{2,1,0:T(8,128)S(1)} %reshape.69) | copy-start | bytes 3145732
  25.4 2.5 %copy-start.8 = (f32[3,3,1024]{2,1,0:T(4,128)S(1)}, f32[3,3,1024]{2,1,0:T(4,128)}, u32[]{:S(2)}) copy-start(f32[3,3,1024]{2,1,0:T(4,128)} %param.11) | copy-start | bytes 110596
  33.5 1.2 %copy-start.1 = (f32[3,128,1024]{1,2,0:T(8,128)}, f32[3,128,1024]{1,2,0:T(8,128)S(1)}, u32[]{:S(2)}) copy-start(f32[3,128,1024]{1,2,0:T(8,128)S(1)} %fusion) | copy-start | bytes 4718596
  35.4 15.7 %all-to-all-start = ((bf16[128,32,32]{0,2,1:T(8,128)(2,1)}), bf16[128,32,32]{0,2,1:T(8,128)(2,1)S(1)}, u32[]{:S(2)}, u32[]{:S(2)}) async-start(bf16[128,32,32]{0,2,1:T(8,128)(2,1)} %bitcast.4), calls=%async_computation | async-start | bytes 524288 | tf_op jit(solution)/shard_map/all_to_all | solution.py:90
  57.3 1.4 %copy-start.3 = (f32[32,128,64]{1,2,0:T(8,128)S(1)}, f32[32,128,64]{1,2,0:T(8,128)}, u32[]{:S(2)}) copy-start(f32[32,128,64]{1,2,0:T(8,128)} %convolution_subtract_fusion.1) | copy-start | bytes 3145732
  57.3 1.5 %copy-start.4 = (f32[32,128,64]{1,2,0:T(8,128)S(1)}, f32[32,128,64]{1,2,0:T(8,128)}, u32[]{:S(2)}) copy-start(f32[32,128,64]{1,2,0:T(8,128)} %convolution_add_fusion.2) | copy-start | bytes 3145732
  69.2 4.8 %copy-start.7 = (bf16[128,1024]{1,0:T(8,128)(2,1)S(1)}, bf16[128,1024]{1,0:T(8,128)(2,1)}, u32[]{:S(2)}) copy-start(bf16[128,1024]{1,0:T(8,128)(2,1)} %param.14) | copy-start | bytes 786436
  69.2 16.5 %copy-start.2 = (f32[3,128,1024]{1,2,0:T(8,128)S(1)}, f32[3,128,1024]{1,2,0:T(8,128)}, u32[]{:S(2)}) copy-start(f32[3,128,1024]{1,2,0:T(8,128)} %copy-done.1) | copy-start | bytes 4718596
  70.1 32.0 %copy-start.9 = (f32[1024]{0:T(1024)S(1)}, f32[1024]{0:T(1024)}, u32[]{:S(2)}) copy-start(f32[1024]{0:T(1024)} %param.15) | copy-start | bytes 12292
  70.1 15.6 %all-to-all-start.1 = ((f32[32,128,32]{1,2,0:T(8,128)}), f32[32,128,32]{1,2,0:T(8,128)S(1)}, u32[]{:S(2)}, u32[]{:S(2)}) async-start(f32[32,128,32]{1,2,0:T(8,128)} %copy_bitcast_fusion), calls=%async_computation.1 | async-start | bytes 1048576 | tf_op jit(solution)/shard_map/all_to_all | solution.py:95
where the time goes:
time: 105 us; the launch traced here: 103 us
  matrix products  31.3 us (30%)
  waiting for transfers between devices  18.2 us (17%)
  blocking collectives  16.2 us (15%)
  starting transfers between devices  15.1 us (14%)
  local copies, waits for them, and re-layouts  13 us (12%)
  other arithmetic  8.92 us (8%)
    dot_general x12, matrix products, mat_out(): jnp.einsum('ckn,nm->ckm', values, table, precision=lax.Precision.HIGHEST)  18 us
    psum x1, blocking collectives, per_device(): squares = lax.psum(jnp.sum(stream * stream, axis=1), 'tp')  16.2 us
    dot_general x6, matrix products, mat_in(): jnp.einsum('kn,cnm->ckm', table, values, precision=lax.Precision.HIGHEST)  13.3 us
    all_to_all x1, waiting for transfers between devices, per_device(): lax.all_to_all(convolved.T, 'ctx', split_axis=0, concat_axis=1, tiled=True)  11.5 us
    all_to_all x1, waiting for transfers between devices, per_device(): lax.all_to_all(gated, 'ctx', split_axis=1, concat_axis=0, tiled=True)  6.7 us
    all_to_all x1, starting transfers between devices, per_device(): lax.all_to_all(gated, 'ctx', split_axis=1, concat_axis=0, tiled=True)  6.69 us
    unnamed x26, local copies, waits for them, and re-layouts  6.35 us
    ppermute x1, starting transfers between devices, from_behind(): return lax.ppermute(block, axis, route)  4.59 us
  transfers between devices with their start and end apart: 3, of which 2 were waited for; matrix products, arithmetic and copies ran while one was open for 20% of the time, Pallas kernels for 0%

commit v1 on v0

v1 whole, which is shorter than its diff:
```python
import functools

import jax
import jax.numpy as jnp
from jax import lax
from jax.experimental import pallas as pl
from jax.experimental.pallas import tpu as pltpu
from jax.sharding import PartitionSpec as P

MESH = pl.DeviceIdType.MESH
D = 8192
ROWS = 128
WIDTH = 1024
LANES = 128
BLOCKS = WIDTH // LANES
MODES = 16
HALF = MODES // 2
TILES = ROWS // 8
F32 = jnp.float32
BF16 = jnp.bfloat16


def lanes_of(b):
    return pl.ds(pl.multiple_of(b * LANES, LANES), LANES)


def short_taps(sf_ref, stream, lanes):
    return [sf_ref[stream, pl.ds(j, 1), lanes] for j in range(3)]


def conv_block(values, taps):
    return taps[0] * values + taps[1] * pltpu.roll(values, 1, 0) + taps[2] * pltpu.roll(values, 2, 0)


def conv_top(values, taps, two_back, one_back):
    row = lax.broadcasted_iota(jnp.int32, values.shape, 0)
    once = jnp.where(row == 0, one_back, pltpu.roll(values, 1, 0))
    twice = jnp.where(row == 0, two_back, jnp.where(row == 1, one_back, pltpu.roll(values, 2, 0)))
    return taps[0] * values + taps[1] * once + taps[2] * twice


def mixer_kernel(
    q_hbm, k_hbm, v_hbm, sf_hbm, rate_hbm, res_hbm, resid_hbm, gain_hbm, out_ref,
    q_s, k_s, v_s, sf_s, rate_s, res_s, resid_s, gain_s,
    edge, halo, step_t, end_t, start_t, u_s, f_s, y_s, qf_s, st_s,
    e_own, e_mate, chip, yb1, xb1, yb2, xb2, zsend, zbuf, sq,
    load_sem, edge_sem, core_sem, y1s, y1r, x1s, x1r, y2s, y2r, x2s, x2r, zs, zr,
):
    ctx = lax.axis_index("ctx")
    tp = lax.axis_index("tp")
    x, y, core = ctx // 8, (ctx // 2) % 4, ctx % 2
    mate = ctx + 1 - 2 * core

    def y_peer(k):
        return x * 8 + ((y + k) % 4) * 2 + core

    def x_peer(k):
        return ((x + k) % 4) * 8 + y * 2 + core

    after, before = (ctx + 1) % 32, (ctx + 31) % 32

    barrier = pltpu.get_barrier_semaphore()
    greeted = [(mate, tp), (after, tp), (before, tp)]
    greeted += [(y_peer(k), tp) for k in (1, 2, 3)] + [(x_peer(k), tp) for k in (1, 2, 3)]
    greeted += [(ctx, (tp + k) % 8) for k in range(1, 8)]
    for who in greeted:
        pl.semaphore_signal(barrier, inc=1, device_id=who, device_id_type=MESH)

    loads = {}
    for i, (name, src, dst) in enumerate([
        ("rate", rate_hbm, rate_s), ("k", k_hbm, k_s), ("v", v_hbm, v_s), ("sf", sf_hbm, sf_s),
        ("q", q_hbm, q_s), ("res", res_hbm, res_s), ("resid", resid_hbm, resid_s), ("gain", gain_hbm, gain_s),
    ]):
        loads[name] = pltpu.make_async_copy(src, dst, load_sem.at[i])
        loads[name].start()

    def remote(src, dst, ssem, rsem, who):
        return pltpu.make_async_remote_copy(
            src_ref=src, dst_ref=dst, send_sem=ssem, recv_sem=rsem, device_id=who, device_id_type=MESH
        )

    loads["rate"].wait()

    @pl.loop(0, BLOCKS)
    def _(b):
        lanes = lanes_of(b)
        row = lax.broadcasted_iota(jnp.int32, (8, LANES), 0).astype(F32)
        for m in range(MODES):
            r = jnp.broadcast_to(rate_s[pl.ds(m, 1), lanes], (8, LANES))
            step_t[m, :, lanes] = jnp.exp(-8.0 * r)
            end_t[m, :, lanes] = jnp.exp((row - 7.0) * r)

    loads["k"].wait()
    loads["v"].wait()
    loads["sf"].wait()
    loads["q"].wait()
    edge[0:2, :] = k_s[ROWS - 16 : ROWS, :].astype(F32)[14:16]
    edge[2:4, :] = v_s[ROWS - 16 : ROWS, :].astype(F32)[14:16]
    edge[4:6, :] = q_s[ROWS - 16 : ROWS, :].astype(F32)[14:16]
    edge[6:8, :] = jnp.zeros((2, WIDTH), F32)

    pl.semaphore_wait(barrier, len(greeted))
    edge_copy = remote(edge, halo, edge_sem.at[0], edge_sem.at[1], (after, tp))
    edge_copy.start()

    @pl.loop(0, BLOCKS)
    def _(b):
        lanes = lanes_of(b)
        kf = conv_block(k_s[:, lanes].astype(F32), short_taps(sf_s, 1, lanes))
        vf = conv_block(v_s[:, lanes].astype(F32), short_taps(sf_s, 2, lanes))
        u = (kf * vf).astype(BF16).astype(F32)
        u_s[b] = u
        row = lax.broadcasted_iota(jnp.int32, (8, LANES), 0)
        step = step_t[:, :, lanes]
        first = jnp.where(row < 2, 0.0, u[0:8])
        g = jnp.broadcast_to(first[None], (MODES, 8, LANES))
        for i in range(1, TILES):
            g = step * g + u[8 * i : 8 * i + 8][None]
        e_own[:, lanes] = jnp.sum(end_t[:, :, lanes] * g, axis=1)

    edge_copy.wait()
    has_before = ctx > 0

    @pl.loop(0, BLOCKS)
    def _(b):
        lanes = lanes_of(b)
        past = jnp.where(has_before, halo[:, lanes], 0.0)
        kf = conv_top(k_s[0:16, lanes].astype(F32)[0:8], short_taps(sf_s, 1, lanes), past[0:1], past[1:2])
        vf = conv_top(v_s[0:16, lanes].astype(F32)[0:8], short_taps(sf_s, 2, lanes), past[2:3], past[3:4])
        u = (kf * vf).astype(BF16).astype(F32)
        u_s[b, 0:8, :] = u
        r = rate_s[:, lanes]
        e_own[:, lanes] = e_own[:, lanes] + jnp.exp(-127.0 * r) * u[0:1] + jnp.exp(-126.0 * r) * u[1:2]

    core_copy = remote(e_own, e_mate, core_sem.at[0], core_sem.at[1], (mate, tp))
    core_copy.start()

    loads["res"].wait()

    @pl.loop(0, BLOCKS)
    def _(b):
        lanes = lanes_of(b)
        row = lax.broadcasted_iota(jnp.int32, (8, LANES), 0).astype(F32)
        terms = []
        for m in range(MODES):
            r = jnp.broadcast_to(rate_s[pl.ds(m, 1), lanes], (8, LANES))
            w = jnp.broadcast_to(res_s[pl.ds(m, 1), lanes], (8, LANES))
            terms.append(w * jnp.exp(-row * r))
            start_t[m, :, lanes] = w * jnp.exp(-(row + 1.0) * r)
        v = jnp.stack(terms)
        step = step_t[:, :, lanes]
        for i in range(TILES):
            f_s[b, 8 * i : 8 * i + 8, :] = jnp.sum(v, axis=0)
            if i < TILES - 1:
                v = v * step

    core_copy.wait()
    rates = rate_s[...]
    one = jnp.exp(-128.0 * rates)
    mine, theirs = e_own[...], e_mate[...]
    first_core = jnp.where(core == 0, mine, theirs)
    second_core = jnp.where(core == 0, theirs, mine)
    chip[...] = one * first_core + second_core
    yb1[y] = chip[0:HALF, :]
    xb1[x] = chip[HALF:MODES, :]
    stage1 = []
    for k in (1, 2, 3):
        stage1.append(remote(chip.at[pl.ds(0, HALF)], yb1.at[y], y1s.at[k], y1r.at[y], (y_peer(k), tp)))
        stage1.append(remote(chip.at[pl.ds(HALF, HALF)], xb1.at[x], x1s.at[k], x1r.at[x], (x_peer(k), tp)))
    for c in stage1:
        c.start()

    def local_conv(b):
        u = u_s[b]
        row = lax.broadcasted_iota(jnp.int32, (8, LANES), 0)
        acc = [None] * TILES
        for shift in range(8):
            if shift == 0:
                moved = u
            else:
                moved = pltpu.roll(u, shift, 0)
                moved = jnp.concatenate([jnp.where(row < shift, 0.0, moved[0:8]), moved[8:]], axis=0)
            for p in range(TILES):
                tap = jnp.broadcast_to(f_s[b, pl.ds(8 * p + shift, 1), :], (8, LANES))
                for i in range(p, TILES):
                    term = tap * moved[8 * (i - p) : 8 * (i - p) + 8]
                    acc[i] = term if acc[i] is None else acc[i] + term
        for i in range(TILES):
            y_s[b, 8 * i : 8 * i + 8, :] = acc[i]

    @pl.loop(0, BLOCKS)
    def _(b):
        lanes = lanes_of(b)
        taps = short_taps(sf_s, 0, lanes)
        values = q_s[:, lanes].astype(F32)
        qf_s[b] = conv_block(values, taps)
        past = jnp.where(has_before, halo[:, lanes], 0.0)
        qf_s[b, 0:8, :] = conv_top(values[0:8], taps, past[4:5], past[5:6])

    @pl.loop(0, BLOCKS // 2)
    def _(b):
        local_conv(b)

    for k in (1, 2, 3):
        remote(chip.at[pl.ds(0, HALF)], yb1.at[(y + k) % 4], y1s.at[k], y1r.at[(y + k) % 4], (y_peer(k), tp)).wait_recv()
        remote(chip.at[pl.ds(0, HALF)], xb1.at[(x + k) % 4], x1s.at[k], x1r.at[(x + k) % 4], (x_peer(k), tp)).wait_recv()

    low, high = rate_s[0:HALF, :], rate_s[HALF:MODES, :]
    by_chip, by_row = jnp.exp(-256.0 * low), jnp.exp(-1024.0 * high)
    total = jnp.zeros((HALF, WIDTH), F32)
    row_part = total
    for i in range(4):
        row_part = jnp.where(y == i, total, row_part)
        total = by_chip * total + yb1[i]
    xb2[x] = total
    run = jnp.zeros((HALF, WIDTH), F32)
    column = run
    for i in range(4):
        column = jnp.where(x == i, run, column)
        run = by_row * run + xb1[i]
    yb2[y] = column
    st_s[0] = total
    st_s[1] = column
    st_s[2] = by_row * column + chip[HALF:MODES, :]
    stage2 = []
    for k in (1, 2, 3):
        stage2.append(remote(st_s.at[0], xb2.at[x], x2s.at[k], x2r.at[x], (x_peer(k), tp)))
        which = 1 + (3 - (y + k) // 4 * 3) // 3
        stage2.append(remote(st_s.at[which], yb2.at[y], y2s.at[k], y2r.at[y], (y_peer(k), tp)))
    for c in stage2:
        c.start()

    @pl.loop(BLOCKS // 2, BLOCKS)
    def _(b):
        local_conv(b)

    for k in (1, 2, 3):
        remote(st_s.at[0], xb2.at[(x + k) % 4], x2s.at[k], x2r.at[(x + k) % 4], (x_peer(k), tp)).wait_recv()
        remote(st_s.at[0], yb2.at[(y + k) % 4], y2s.at[k], y2r.at[(y + k) % 4], (y_peer(k), tp)).wait_recv()

    by_row_low = jnp.exp(-1024.0 * low)
    run = jnp.zeros((HALF, WIDTH), F32)
    rows_before = run
    for i in range(4):
        rows_before = jnp.where(x == i, run, rows_before)
        if i < 3:
            run = by_row_low * run + xb2[i]
    state_low = row_part + jnp.exp((-256.0 * y.astype(F32)) * low) * rows_before
    state_high = jnp.zeros((HALF, WIDTH), F32)
    for i in range(4):
        gap = ((y + 3 - i) % 4).astype(F32)
        state_high = state_high + jnp.exp((-256.0 * gap) * high) * yb2[i]
    state = jnp.concatenate([state_low, state_high], axis=0)
    state = jnp.where(core == 0, state, jnp.exp(-128.0 * rate_s[...]) * state + e_mate[...])
    e_own[...] = state

    loads["resid"].wait()
    sq[...] = jnp.zeros((ROWS, LANES), F32)

    @pl.loop(0, BLOCKS)
    def _(b):
        lanes = lanes_of(b)
        step = step_t[:, :, lanes]
        v = jnp.stack([
            start_t[m, :, lanes] * jnp.broadcast_to(e_own[pl.ds(m, 1), lanes], (8, LANES)) for m in range(MODES)
        ])
        for i in range(TILES):
            tile = pl.ds(8 * i, 8)
            mixed = y_s[b, tile, :] + jnp.sum(v, axis=0)
            if i < TILES - 1:
                v = v * step
            qf_s[b, tile, :] = qf_s[b, tile, :] * mixed
        stream = resid_s[:, lanes].astype(F32) + qf_s[b]
        y_s[b] = stream
        sq[...] = sq[...] + stream * stream

    ones = jnp.ones((8, LANES), F32)
    contract_lanes = (((1,), (1,)), ((), ()))
    sums = lax.dot_general(ones, sq[...], contract_lanes, precision=lax.Precision.HIGHEST, preferred_element_type=F32)
    zsend[...] = sums[0:1]
    zbuf[tp] = sums[0:1]
    zcopies = [
        remote(zsend, zbuf.at[tp], zs.at[k], zr.at[tp], (ctx, (tp + k) % 8)) for k in range(1, 8)
    ]
    for c in zcopies:
        c.start()
    loads["gain"].wait()
    for k in range(1, 8):
        remote(zsend, zbuf.at[(tp + k) % 8], zs.at[k], zr.at[(tp + k) % 8], (ctx, (tp + k) % 8)).wait_recv()
    parts = jnp.concatenate([zbuf[i] for i in range(8)], axis=0)
    squares = lax.dot_general(
        parts, ones, (((0,), (0,)), ((), ())), precision=lax.Precision.HIGHEST, preferred_element_type=F32
    )
    scale = lax.rsqrt(squares * (1.0 / D) + 1e-05)
    sq[...] = scale

    @pl.loop(0, BLOCKS)
    def _(b):
        lanes = lanes_of(b)
        out_ref[:, lanes] = (y_s[b] * sq[...] * gain_s[:, lanes]).astype(BF16)

    for c in stage1 + stage2 + zcopies:
        c.wait_send()


def per_device(q_in, k_in, v_in, short_filter, rate, residue, resid, gain):
    vm = pltpu.VMEM
    dma = pltpu.SemaphoreType.DMA
    any_spec = pl.BlockSpec(memory_space=pltpu.HBM)
    stream = (ROWS, WIDTH)
    table = (MODES, 8, WIDTH)
    blocks = (BLOCKS, ROWS, LANES)
    half4 = (4, HALF, WIDTH)
    return pl.pallas_call(
        mixer_kernel,
        out_shape=jax.ShapeDtypeStruct(stream, BF16),
        in_specs=[any_spec] * 8,
        out_specs=pl.BlockSpec(memory_space=pltpu.VMEM),
        scratch_shapes=[
            vm(stream, BF16), vm(stream, BF16), vm(stream, BF16), vm((3, 3, WIDTH), F32),
            vm((MODES, WIDTH), F32), vm((MODES, WIDTH), F32), vm(stream, BF16), vm((1, WIDTH), F32),
            vm((8, WIDTH), F32), vm((8, WIDTH), F32), vm(table, F32), vm(table, F32), vm(table, F32),
            vm(blocks, F32), vm(blocks, F32), vm(blocks, F32), vm(blocks, F32), vm((3, HALF, WIDTH), F32),
            vm((MODES, WIDTH), F32), vm((MODES, WIDTH), F32), vm((MODES, WIDTH), F32),
            vm(half4, F32), vm(half4, F32), vm(half4, F32), vm(half4, F32),
            vm((1, LANES), F32), vm((8, 1, LANES), F32), vm((ROWS, LANES), F32),
            dma((8,)), dma((2,)), dma((2,)),
            dma((4,)), dma((4,)), dma((4,)), dma((4,)), dma((4,)), dma((4,)), dma((4,)), dma((4,)),
            dma((8,)), dma((8,)),
        ],
        compiler_params=pltpu.CompilerParams(
            collective_id=0, has_side_effects=True, vmem_limit_bytes=48 * 1024 * 1024
        ),
        name="mixer",
    )(q_in, k_in, v_in, short_filter, rate.T, residue.T, resid, gain.reshape(1, WIDTH))


def solution(mesh):
    in_specs = (
        P("ctx", "tp"),
        P("ctx", "tp"),
        P("ctx", "tp"),
        P(None, None, "tp"),
        P("tp", None),
        P("tp", None),
        P("ctx", "tp"),
        P("tp"),
    )
    return jax.shard_map(
        per_device, mesh=mesh, in_specs=in_specs, out_specs=P("ctx", "tp"), check_vma=False
    )
```

time: 105 us -> 35.4 us (0.34); the launches traced: 103 us -> 35 us
  matrix products: 31.3 us -> 0 us
  Pallas kernels: 0 us -> 27.4 us
  waiting for transfers between devices: 18.2 us -> 0 us
  blocking collectives: 16.2 us -> 0 us
  starting transfers between devices: 15.1 us -> 0 us
  other arithmetic: 8.92 us -> 0 us
  local copies, waits for them, and re-layouts: 13 us -> 7.67 us
    dot_general x18 -> x0, matrix products: 31.3 us -> none  [the longest x12 18 us: mat_out(): jnp.einsum('ckn,nm->ckm', values, table, precision=lax.Precision.HIGHEST)]
    pallas_call x0 -> x1, Pallas kernels: none -> 27.4 us  [per_device(): pl.pallas_call(mixer_kernel, out_shape=jax.ShapeDtypeStruct(stream, BF16)...]
    all_to_all x2 -> x0, waiting for transfers between devices: 18.2 us -> none  [the longest x1 11.5 us: per_device(): lax.all_to_all(convolved.T, 'ctx', split_axis=0, concat_axis=1, tiled=True)]
    psum x1 -> x0, blocking collectives: 16.2 us -> none  [per_device(): squares = lax.psum(jnp.sum(stream * stream, axis=1), 'tp')]
    all_to_all x2 -> x0, starting transfers between devices: 10.5 us -> none  [the longest x1 6.69 us: per_device(): lax.all_to_all(gated, 'ctx', split_axis=1, concat_axis=0, tiled=True)]
    ppermute x1 -> x0, starting transfers between devices: 4.59 us -> none  [from_behind(): return lax.ppermute(block, axis, route)]
    add x2 -> x0, other arithmetic: 3.98 us -> none  [the longest x1 2.35 us: per_device(): feats + short_filter[:, j, None, :] * padded[:, taps - 1 - j:taps - 1 - j...]
    convert_element_type x4 -> x0, other arithmetic: 2.86 us -> none  [the longest x1 1.9 us: per_device(): padded = jnp.concatenate([before, stacked], axis=1).astype(jnp.float32)]
  transfers between devices with their start and end apart: 3 -> 0, of which waited for: 2 -> 0; matrix products, arithmetic and copies ran while one was open for 20% -> 0% of each run, Pallas kernels for 0% -> 0%
where the time goes in v1:
time: 35.4 us; the launch traced here: 35 us
  Pallas kernels  27.4 us (77%)
  local copies, waits for them, and re-layouts  7.67 us (22%)
    pallas_call x1, Pallas kernels, per_device(): pl.pallas_call(mixer_kernel, out_shape=jax.ShapeDtypeStruct(stream, BF16)...  27.4 us
    unnamed x17, local copies, waits for them, and re-layouts  7.67 us

profile of v1, /device:TPU:1, one launch (start us, length us, event | category | flops | bytes accessed | tf_op | source)
XLA Modules:
  0.0 35.0 jit_solution(3428515081804745073)
XLA Ops:
  0.0 0.0 copy-start.7
  0.0 0.7 %copy-done.7 = f32[1024]{0:T(1024)S(1)} copy-done((f32[1024]{0:T(1024)S(1)}, f32[1024]{0:T(1024)}, u32[]{:S(2)}) %copy-start.7) | copy-done | bytes 4120
  0.7 0.0 copy-start
  0.7 0.9 %copy-done = bf16[128,1024]{1,0:T(8,128)(2,1)S(1)} copy-done((bf16[128,1024]{1,0:T(8,128)(2,1)S(1)}, bf16[128,1024]{1,0:T(8,128)(2,1)}, u32[]{:S(2)}) %copy-start) | copy-done | bytes 262168
  1.6 0.0 copy-start.1
  1.6 0.9 %copy-done.1 = bf16[128,1024]{1,0:T(8,128)(2,1)S(1)} copy-done((bf16[128,1024]{1,0:T(8,128)(2,1)S(1)}, bf16[128,1024]{1,0:T(8,128)(2,1)}, u32[]{:S(2)}) %copy-start.1) | copy-done | bytes 262168
  2.6 0.0 copy-start.2
  2.6 0.9 %copy-done.2 = bf16[128,1024]{1,0:T(8,128)(2,1)S(1)} copy-done((bf16[128,1024]{1,0:T(8,128)(2,1)S(1)}, bf16[128,1024]{1,0:T(8,128)(2,1)}, u32[]{:S(2)}) %copy-start.2) | copy-done | bytes 262168
  3.5 0.0 copy-start.3
  3.5 0.9 %copy-done.3 = bf16[128,1024]{1,0:T(8,128)(2,1)S(1)} copy-done((bf16[128,1024]{1,0:T(8,128)(2,1)S(1)}, bf16[128,1024]{1,0:T(8,128)(2,1)}, u32[]{:S(2)}) %copy-start.3) | copy-done | bytes 262168
  4.5 0.0 copy-start.4
  4.5 0.8 %copy-done.4 = f32[1024,16]{0,1:T(8,128)S(1)} copy-done((f32[1024,16]{0,1:T(8,128)S(1)}, f32[1024,16]{0,1:T(8,128)}, u32[]{:S(2)}) %copy-start.4) | copy-done | bytes 65560
  5.3 0.0 copy-start.5
  5.3 0.8 %copy-done.5 = f32[1024,16]{0,1:T(8,128)S(1)} copy-done((f32[1024,16]{0,1:T(8,128)S(1)}, f32[1024,16]{0,1:T(8,128)}, u32[]{:S(2)}) %copy-start.5) | copy-done | bytes 65560
  6.2 0.0 copy-start.6
  6.2 0.8 %copy-done.6 = f32[3,3,1024]{2,1,0:T(4,128)S(1)} copy-done((f32[3,3,1024]{2,1,0:T(4,128)S(1)}, f32[3,3,1024]{2,1,0:T(4,128)}, u32[]{:S(2)}) %copy-start.6) | copy-done | bytes 36888
  7.0 27.4 %mixer.1 = bf16[128,1024]{1,0:T(8,128)(2,1)S(1)} custom-call(bf16[128,1024]{1,0:T(8,128)(2,1)S(1)} %copy-done, bf16[128,1024]{1,0:T(8,128)(2,1)S(1)} %copy-done.1, bf16[128,1024]{1,0:T(8,128)(2,1)S(1)} %copy-done.2, f32[3,3,1024]{2,1,0:T(4,128)S(1)} %copy-done.6, f32[16,1024]{1,0:T(8,128)S(1)} %bitcast.3, f32[16,1024]{1,0:T(8,128)S(1)} %bitcast.4, ...), custom_call_target="tpu_custom_call" | custom-call | tf_op jit(solution)/shard_map/mixer/pallas_call | solution.py:314
  34.3 0.7 %copy.10 = bf16[128,1024]{1,0:T(8,128)(2,1)} copy(bf16[128,1024]{1,0:T(8,128)(2,1)S(1)} %mixer.1) | data formatting | bytes 524288
Async XLA Ops:
  0.0 0.7 %copy-start.7 = (f32[1024]{0:T(1024)S(1)}, f32[1024]{0:T(1024)}, u32[]{:S(2)}) copy-start(f32[1024]{0:T(1024)} %param.15) | copy-start | bytes 12292
  0.7 0.9 %copy-start = (bf16[128,1024]{1,0:T(8,128)(2,1)S(1)}, bf16[128,1024]{1,0:T(8,128)(2,1)}, u32[]{:S(2)}) copy-start(bf16[128,1024]{1,0:T(8,128)(2,1)} %q_hbm.1) | copy-start | bytes 786436
  1.6 0.9 %copy-start.1 = (bf16[128,1024]{1,0:T(8,128)(2,1)S(1)}, bf16[128,1024]{1,0:T(8,128)(2,1)}, u32[]{:S(2)}) copy-start(bf16[128,1024]{1,0:T(8,128)(2,1)} %k_hbm.1) | copy-start | bytes 786436
  2.6 0.9 %copy-start.2 = (bf16[128,1024]{1,0:T(8,128)(2,1)S(1)}, bf16[128,1024]{1,0:T(8,128)(2,1)}, u32[]{:S(2)}) copy-start(bf16[128,1024]{1,0:T(8,128)(2,1)} %v_hbm.1) | copy-start | bytes 786436
  3.5 0.9 %copy-start.3 = (bf16[128,1024]{1,0:T(8,128)(2,1)S(1)}, bf16[128,1024]{1,0:T(8,128)(2,1)}, u32[]{:S(2)}) copy-start(bf16[128,1024]{1,0:T(8,128)(2,1)} %resid_hbm.1) | copy-start | bytes 786436
  4.5 0.8 %copy-start.4 = (f32[1024,16]{0,1:T(8,128)S(1)}, f32[1024,16]{0,1:T(8,128)}, u32[]{:S(2)}) copy-start(f32[1024,16]{0,1:T(8,128)} %param.12) | copy-start | bytes 196612
  5.3 0.8 %copy-start.5 = (f32[1024,16]{0,1:T(8,128)S(1)}, f32[1024,16]{0,1:T(8,128)}, u32[]{:S(2)}) copy-start(f32[1024,16]{0,1:T(8,128)} %param.13) | copy-start | bytes 196612
  6.2 0.8 %copy-start.6 = (f32[3,3,1024]{2,1,0:T(4,128)S(1)}, f32[3,3,1024]{2,1,0:T(4,128)}, u32[]{:S(2)}) copy-start(f32[3,3,1024]{2,1,0:T(4,128)} %sf_hbm.1) | copy-start | bytes 110596
